TPU v7x, 32 devices: a whole 2x2x4 slice. The times are simulated.
32 devices in a mesh: groups: 2 (over y), lat: 4 (over z), lev: 2 (over x), tr: 2 (over core).
Axes of the slice: x: 2, y: 2, z: 4, core: 2. Of those that a mesh axis runs over, the one named last changes fastest.
Arguments:
- adjoint_in: float32 [4, 24, 32, 512], P(('groups', 'tr'), 'lev', 'lat'), parts along dimension 0, may hold values from -6 to 6
- courant: float32 [2, 24, 32, 512], P(None, 'lev', 'lat'), may hold values from -0.45 to 0.45
- diffusion: float32 [23, 32, 512], P(None, 'lat', 'lev'), may hold values from 0.3 to 6
- tile_values: float32 [4, 24, 256, 128], P(('groups', 'tr'), 'lev', 'lat'), parts along dimension 0, may hold values from -6 to 6
- tile_region: int32 [512, 1], P(('groups', 'lat')), parts along dimension 0, may hold values from 0 to 3; in each aligned block of 64 rows (0 to 63, 64 to 127, ...) at most 16 rows name the same one
- tile_cell: int32 [512], P(('groups', 'lat')), parts along dimension 0, may hold values from 0 to 31
Outputs:
- adjoint_out: float32 [4, 24, 32, 512], P(('groups', 'tr'), 'lev', 'lat'), parts along dimension 0
- flux_gradient: float32 [4, 32, 512], P(('groups', 'tr'), 'lat', 'lev'), parts along dimension 0
There are 2 independent parts, one for each index of `groups`. A program takes and returns all parts, laid end to end along the dimension named above; an argument that names none is the same for every part. Nothing has to cross between parts.
Inputs may be any that keep to these rules, and one draw needn't show every extreme that they name: `tile_region`: among the tiles of one index of lat (aligned blocks of 64 tiles) at most 16 name any one band, a bound that some block reaches of them.
All inputs are finite; a program needn't handle non-finite values.
Results may differ from a plain program's by a relative error of at most 0.0001.
Values sent between devices are 32-bit elements; how exact they have to be, the bound alone decides.
No kernel may reach another device: no remote copies, remote signals or barrier semaphores. Data moves between devices by JAX's collectives and lax.ppermute only.
A program may use at most 64 MiB of HBM per device.

v0:
```python
import functools

import jax
import jax.numpy as jnp
from jax import lax
from jax.experimental import pallas as pl
from jax.experimental.pallas import tpu as pltpu
from jax.sharding import PartitionSpec as P

STEPS = 6
F32 = jnp.float32


def call(body, out_shapes, *args):
    spec = pl.BlockSpec(memory_space=pltpu.VMEM)
    return pl.pallas_call(
        body,
        out_shape=[jax.ShapeDtypeStruct(shape, F32) for shape in out_shapes],
        in_specs=[spec] * len(args),
        out_specs=[spec] * len(out_shapes),
        compiler_params=pltpu.CompilerParams(vmem_limit_bytes=24 * 1024 * 1024),
    )(*args)


def order(i, count, upper):
    return jnp.where(upper, i, count - 1 - i)


def upper_half(devices):
    return lax.axis_index("lev") < devices // 2


def prepare_body(devices, field, window, courant, face_north, gain_in, y_in, *outs):
    r_out, a_out, g_out, me_out, mw_out, ze_out, zw_out, y_out, ends_out = outs
    count, rows, width = field.shape
    upper = upper_half(devices)
    row = lax.broadcasted_iota(jnp.int32, (rows, width), 0)
    first_row = (row == 0) & (lax.axis_index("lat") == 0)
    gain, y = gain_in[...], y_in[...]
    for i in range(count):
        level = order(i, count, upper)
        k_prev = window[jnp.where(upper, i, count - i)]
        k_next = window[jnp.where(upper, i + 1, count - 1 - i)]
        inverse = 1.0 / (1.0 + k_prev + k_next - k_prev * gain)
        gain = k_next * inverse
        a = k_prev * inverse
        r_out[i], a_out[i], g_out[i] = inverse, a, gain
        y = field[level] * inverse + a * y
        y_out[i] = y
        south = courant[1, level]
        north = pltpu.roll(south, rows - 1, 0)
        north = jnp.where(row == rows - 1, face_north[pl.ds(level, 1), :], north)
        me_out[i] = jnp.maximum(north, 0.0)
        mw_out[i] = jnp.where(first_row, 0.0, jnp.minimum(south, 0.0))
        west = courant[0, level]
        ze_out[i] = jnp.maximum(pltpu.roll(west, width - 1, 1), 0.0)
        zw_out[i] = jnp.minimum(west, 0.0)
    ends_out[0] = y
    ends_out[1] = gain


def back_body(devices, first, *refs):
    if first:
        y, other, g, lam, south, north, flux, scale_out = refs
    else:
        y, other, g, scale, flux_in, lam, south, north, flux = refs
    count, rows, _ = y.shape
    last = count - 1
    if first:
        at = lax.axis_index("lev")
        middle = (at == devices // 2) | (at == devices // 2 - 1)
        scale = jnp.where(middle, 1.0 / (1.0 - g[last] * other[1]), 1.0)
        scale_out[...] = scale
        met = other[0]
    else:
        scale = scale[...]
        met = other[...]
    w = (y[last] + g[last] * met) * scale
    for i in range(last, -1, -1):
        if i < last:
            w = y[i] + g[i] * w
        lam[i] = w
        south[pl.ds(i, 1), :] = w[0:1, :]
        north[pl.ds(i, 1), :] = w[rows - 1 : rows, :]
    flux[...] = w if first else flux_in[...] + w


def advect(i, lam, below, above, me, mw, ze, zw):
    _, rows, width = lam.shape
    row = lax.broadcasted_iota(jnp.int32, (rows, width), 0)
    v = lam[i]
    up = jnp.where(row == rows - 1, above[pl.ds(i, 1), :], pltpu.roll(v, rows - 1, 0))
    down = jnp.where(row == 0, below[pl.ds(i, 1), :], pltpu.roll(v, 1, 0))
    v = v + me[i] * (up - v) + mw[i] * (v - down)
    east = pltpu.roll(v, width - 1, 1)
    west = pltpu.roll(v, 1, 1)
    return v + ze[i] * (east - v) + zw[i] * (v - west)


def forward_body(lam, below, above, me, mw, ze, zw, r, a, y_in, y_out, end_out):
    y = y_in[...]
    for i in range(lam.shape[0]):
        y = advect(i, lam, below, above, me, mw, ze, zw) * r[i] + a[i] * y
        y_out[i] = y
    end_out[...] = y


def finish_body(devices, lam, below, above, me, mw, ze, zw, *rest):
    buckets, out = rest[:-1], rest[-1]
    count, rows, width = lam.shape
    upper = upper_half(devices)
    cells = jnp.concatenate([bucket[count] for bucket in buckets], axis=0)
    tile = cells.shape[1]
    blocks = width // tile
    lane = lax.broadcasted_iota(jnp.int32, cells.shape, 1)
    place = (lane % rows * blocks + lane // rows).astype(F32)
    hits = jnp.where((cells == place) & (lane < rows * blocks), 1.0, 0.0)
    hits = hits.T[: rows * blocks]
    for i in range(count):
        level = order(i, count, upper)
        v = advect(i, lam, below, above, me, mw, ze, zw)
        values = jnp.concatenate([bucket[level] for bucket in buckets], axis=0)
        added = lax.dot_general(
            hits, values, (((1,), (0,)), ((), ())), precision=lax.Precision.HIGHEST, preferred_element_type=F32
        )
        for block in range(blocks):
            out[level, :, block * tile : (block + 1) * tile] = (
                v[:, block * tile : (block + 1) * tile] + added[block * rows : (block + 1) * rows]
            )


def bucket_body(regions, values, region_column, region_row, cell_column, *outs):
    count, tiles, tile = values.shape
    capacity = outs[0].shape[1]
    band = lax.axis_index("lat")
    earlier = lax.broadcasted_iota(jnp.int32, (tiles, tiles), 0) < lax.broadcasted_iota(jnp.int32, (tiles, tiles), 1)
    same = (region_column[...] == region_row[...]) & earlier
    rank = jnp.sum(jnp.where(same, 1.0, 0.0), axis=0, keepdims=True).astype(jnp.int32)
    slot = lax.broadcasted_iota(jnp.int32, (capacity, tiles), 0)
    cells = jnp.broadcast_to(cell_column[...].astype(F32), (tiles, tile))
    picks = [
        jnp.where((slot == rank) & (region_row[...] == lax.rem(band + s, regions)), 1.0, 0.0) for s in range(regions)
    ]
    picks = jnp.concatenate(picks, axis=0)
    for level in range(count + 1):
        got = lax.dot_general(
            picks,
            cells if level == count else values[level],
            (((1,), (0,)), ((), ())),
            precision=lax.Precision.HIGHEST,
            preferred_element_type=F32,
        )
        for s in range(regions):
            outs[s][level] = got[s * capacity : (s + 1) * capacity]


def route_tiles(tile_values, tile_region, tile_cell):
    regions = lax.axis_size("lat")
    count, tiles, tile = tile_values.shape
    outs = call(
        functools.partial(bucket_body, regions),
        [(count + 1, tiles // 4, tile)] * regions,
        tile_values,
        tile_region,
        tile_region.reshape(1, tiles),
        tile_cell.reshape(tiles, 1),
    )
    got = [outs[0]]
    for s in range(1, regions):
        got.append(lax.ppermute(outs[s], "lat", [(b, (b + s) % regions) for b in range(regions)]))
    return got


def diffusion_window(diffusion, count):
    devices = lax.axis_size("lev")
    at = lax.axis_index("lev")
    chunk = diffusion.shape[2]
    padded = jnp.pad(diffusion, ((1, 1), (0, 0), (0, 0)))
    parts = []
    for shift in range(devices):
        target = lax.rem(at + shift, devices)
        part = lax.dynamic_slice_in_dim(padded, target * count, count + 1, axis=0)
        if shift:
            part = lax.ppermute(part, "lev", [(p, (p + shift) % devices) for p in range(devices)])
        parts.append(part)
    parts = jnp.stack(parts)
    return jnp.concatenate([parts[(at - p) % devices] for p in range(devices)], axis=2)


def local(adjoint_in, courant, diffusion, tile_values, tile_region, tile_cell):
    field = adjoint_in[0]
    count, rows, width = field.shape
    devices = lax.axis_size("lev")
    bands = lax.axis_size("lat")
    half = devices // 2
    at = lax.axis_index("lev")
    outermost = (at == 0) | (at == devices - 1)
    innermost = (at == half) | (at == half - 1)
    inward = [(p, p + 1) for p in range(half - 1)] + [(p, p - 1) for p in range(half + 1, devices)]
    outward = [(b, a) for a, b in inward]
    meet = [(half - 1, half), (half, half - 1)]
    northward = [(b, b + 1) for b in range(bands - 1)]
    southward = [(b + 1, b) for b in range(bands - 1)]

    buckets = route_tiles(tile_values[0], tile_region, tile_cell)
    window = diffusion_window(diffusion, count)
    face_north = lax.ppermute(courant[1, :, 0, :], "lat", southward)

    whole, plane, edge = (count, rows, width), (rows, width), (count, width)
    zero = jnp.zeros(plane, F32)
    gain_in, y_in = zero, zero
    for turn in range(half):
        r, a, g, me, mw, ze, zw, y, ends = call(
            functools.partial(prepare_body, devices),
            [whole] * 8 + [(2,) + plane],
            field,
            window,
            courant,
            face_north,
            gain_in,
            y_in,
        )
        if turn < half - 1:
            passed = jnp.where(outermost, 0.0, lax.ppermute(ends, "lev", inward))
            y_in, gain_in = passed[0], passed[1]

    for step in range(STEPS):
        met = lax.ppermute(ends, "lev", meet)
        for turn in range(half):
            if step == 0:
                lam, south, north, new_flux, scale = call(
                    functools.partial(back_body, devices, True), [whole, edge, edge, plane, plane], y, met, g
                )
            else:
                lam, south, north, new_flux = call(
                    functools.partial(back_body, devices, False),
                    [whole, edge, edge, plane],
                    y,
                    met,
                    g,
                    scale,
                    flux,
                )
            if turn < half - 1:
                passed = lax.ppermute(lam[0], "lev", outward)
                if step == 0:
                    passed = jnp.stack([passed, jnp.zeros_like(passed)])
                met = jnp.where(innermost, met, passed)
        flux = new_flux
        below = lax.ppermute(north, "lat", northward)
        above = lax.ppermute(south, "lat", southward)
        args = (lam, below, above, me, mw, ze, zw)
        if step == STEPS - 1:
            (out,) = call(functools.partial(finish_body, devices), [whole], *args, *buckets)
            break
        y_in = zero
        for turn in range(half):
            y, ends = call(forward_body, [whole, plane], *args, r, a, y_in)
            if turn < half - 1:
                y_in = jnp.where(outermost, 0.0, lax.ppermute(ends, "lev", inward))

    flux = flux / STEPS
    chunk = width // devices
    share = flux[:, :chunk]
    for p in range(1, devices):
        sent = lax.ppermute(flux[:, p * chunk : (p + 1) * chunk], "lev", [(0, p)])
        share = jnp.where(at == p, sent, share)
    return out[None], share[None]


def solution(mesh):
    return jax.shard_map(
        local,
        mesh=mesh,
        in_specs=(
            P(("groups", "tr"), "lev", "lat", None),
            P(None, "lev", "lat", None),
            P(None, "lat", "lev"),
            P(("groups", "tr"), "lev", "lat", None),
            P(("groups", "lat"), None),
            P(("groups", "lat")),
        ),
        out_specs=(P(("groups", "tr"), "lev", "lat", None), P(("groups", "tr"), "lat", "lev")),
        check_vma=False,
    )
```

profile of v0, /device:TPU:0, one launch (start us, length us, event | category | flops | bytes accessed | tf_op | source)
XLA Modules:
  0.0 96.8 jit_solution(16191868911250130006)
XLA Ops:
  1.7 3.0 %collective-permute-start = (f32[13,8,256]{2,1,0:T(8,128)S(1)}, f32[13,8,256]{2,1,0:T(8,128)S(1)}, u32[]{:S(2)}, u32[]{:S(2)}) collective-permute-start(f32[13,8,256]{2,1,0:T(8,128)S(1)} %get-tuple-element.100), channel_id=1, source_target_pairs={{0,2},{2,0},{1,3},{3,1},{4,6},{6,4},{5,7},{7,5},{8,10},{10,8},{9,1... | collective-permute-start | bytes 319496 | tf_op jit(solution)/shard_map/ppermute | solution.py:184
  4.7 1.3 %collective-permute-start.1 = (f32[12,512]{1,0:T(8,128)S(1)}, f32[12,512]{1,0:T(8,128)S(1)}, u32[]{:S(2)}, u32[]{:S(2)}) collective-permute-start(f32[12,512]{1,0:T(8,128)S(1)} %bitcast.22), channel_id=1, source_target_pairs={{4,0},{8,4},{12,8},{5,1},{9,5},{13,9},{6,2},{10,6},{14,10},{7,3},{... | collective-permute-start | bytes 73736 | tf_op jit(solution)/shard_map/ppermute | solution.py:207
  6.0 1.6 %collective-permute-done = f32[13,8,256]{2,1,0:T(8,128)S(1)} collective-permute-done((f32[13,8,256]{2,1,0:T(8,128)S(1)}, f32[13,8,256]{2,1,0:T(8,128)S(1)}, u32[]{:S(2)}, u32[]{:S(2)}) %collective-permute-start) | collective-permute-done | bytes 106528 | tf_op jit(solution)/shard_map/ppermute | solution.py:184
  7.7 2.8 %collective-permute-done.1.face_north = f32[12,512]{1,0:T(8,128)S(1)} collective-permute-done((f32[12,512]{1,0:T(8,128)S(1)}, f32[12,512]{1,0:T(8,128)S(1)}, u32[]{:S(2)}, u32[]{:S(2)}) %collective-permute-start.1) | collective-permute-done | bytes 24608 | tf_op jit(solution)/shard_map/ppermute | solution.py:207
  10.8 3.8 %collective-permute-done.2.refs_1_ = f32[2,8,512]{2,1,0:T(8,128)S(1)} collective-permute-done((f32[2,8,512]{2,1,0:T(8,128)S(1)}, f32[2,8,512]{2,1,0:T(8,128)S(1)}, u32[]{:S(2)}, u32[]{:S(2)}) %collective-permute-start.2) | collective-permute-done | bytes 32800 | tf_op jit(solution)/shard_map/ppermute | solution.py:228
  14.7 3.5 %collective-permute-start.3 = (f32[12,512]{1,0:T(8,128)S(1)}, f32[12,512]{1,0:T(8,128)S(1)}, u32[]{:S(2)}, u32[]{:S(2)}) collective-permute-start(f32[12,512]{1,0:T(8,128)S(1)} %get-tuple-element.54), channel_id=1, source_target_pairs={{0,4},{4,8},{8,12},{1,5},{5,9},{9,13},{2,6},{6,10},{10,14},{3,7},{... | collective-permute-start | bytes 73736 | tf_op jit(solution)/shard_map/ppermute | solution.py:250
  18.2 1.3 %collective-permute-start.4 = (f32[12,512]{1,0:T(8,128)S(1)}, f32[12,512]{1,0:T(8,128)S(1)}, u32[]{:S(2)}, u32[]{:S(2)}) collective-permute-start(f32[12,512]{1,0:T(8,128)S(1)} %get-tuple-element.55), channel_id=1, source_target_pairs={{4,0},{8,4},{12,8},{5,1},{9,5},{13,9},{6,2},{10,6},{14,10},{7,3},{... | collective-permute-start | bytes 73736 | tf_op jit(solution)/shard_map/ppermute | solution.py:251
  19.8 4.2 %collective-permute-done.4.above = f32[12,512]{1,0:T(8,128)S(1)} collective-permute-done((f32[12,512]{1,0:T(8,128)S(1)}, f32[12,512]{1,0:T(8,128)S(1)}, u32[]{:S(2)}, u32[]{:S(2)}) %collective-permute-start.4) | collective-permute-done | bytes 24608 | tf_op jit(solution)/shard_map/ppermute | solution.py:251
  24.8 3.2 %collective-permute-done.5.refs_1_ = f32[8,512]{1,0:T(8,128)S(1)} collective-permute-done((f32[8,512]{1,0:T(8,128)S(1)}, f32[8,512]{1,0:T(8,128)S(1)}, u32[]{:S(2)}, u32[]{:S(2)}) %collective-permute-start.5) | collective-permute-done | bytes 16416 | tf_op jit(solution)/shard_map/ppermute | solution.py:228
  28.1 3.5 %collective-permute-start.6 = (f32[12,512]{1,0:T(8,128)S(1)}, f32[12,512]{1,0:T(8,128)S(1)}, u32[]{:S(2)}, u32[]{:S(2)}) collective-permute-start(f32[12,512]{1,0:T(8,128)S(1)} %get-tuple-element.67), channel_id=1, source_target_pairs={{0,4},{4,8},{8,12},{1,5},{5,9},{9,13},{2,6},{6,10},{10,14},{3,7},{... | collective-permute-start | bytes 73736 | tf_op jit(solution)/shard_map/ppermute | solution.py:250
  31.5 1.3 %collective-permute-start.7 = (f32[12,512]{1,0:T(8,128)S(1)}, f32[12,512]{1,0:T(8,128)S(1)}, u32[]{:S(2)}, u32[]{:S(2)}) collective-permute-start(f32[12,512]{1,0:T(8,128)S(1)} %get-tuple-element.68), channel_id=1, source_target_pairs={{4,0},{8,4},{12,8},{5,1},{9,5},{13,9},{6,2},{10,6},{14,10},{7,3},{... | collective-permute-start | bytes 73736 | tf_op jit(solution)/shard_map/ppermute | solution.py:251
  33.1 4.2 %collective-permute-done.7.above = f32[12,512]{1,0:T(8,128)S(1)} collective-permute-done((f32[12,512]{1,0:T(8,128)S(1)}, f32[12,512]{1,0:T(8,128)S(1)}, u32[]{:S(2)}, u32[]{:S(2)}) %collective-permute-start.7) | collective-permute-done | bytes 24608 | tf_op jit(solution)/shard_map/ppermute | solution.py:251
  38.1 3.2 %collective-permute-done.8.refs_1_ = f32[8,512]{1,0:T(8,128)S(1)} collective-permute-done((f32[8,512]{1,0:T(8,128)S(1)}, f32[8,512]{1,0:T(8,128)S(1)}, u32[]{:S(2)}, u32[]{:S(2)}) %collective-permute-start.8) | collective-permute-done | bytes 16416 | tf_op jit(solution)/shard_map/ppermute | solution.py:228
  41.4 1.3 %collective-permute-start.10 = (f32[12,512]{1,0:T(8,128)S(1)}, f32[12,512]{1,0:T(8,128)S(1)}, u32[]{:S(2)}, u32[]{:S(2)}) collective-permute-start(f32[12,512]{1,0:T(8,128)S(1)} %get-tuple-element.74), channel_id=1, source_target_pairs={{4,0},{8,4},{12,8},{5,1},{9,5},{13,9},{6,2},{10,6},{14,10},{7,3},{... | collective-permute-start | bytes 73736 | tf_op jit(solution)/shard_map/ppermute | solution.py:251
  42.7 4.5 %collective-permute-start.9 = (f32[12,512]{1,0:T(8,128)S(1)}, f32[12,512]{1,0:T(8,128)S(1)}, u32[]{:S(2)}, u32[]{:S(2)}) collective-permute-start(f32[12,512]{1,0:T(8,128)S(1)} %get-tuple-element.73), channel_id=1, source_target_pairs={{0,4},{4,8},{8,12},{1,5},{5,9},{9,13},{2,6},{6,10},{10,14},{3,7},{... | collective-permute-start | bytes 73736 | tf_op jit(solution)/shard_map/ppermute | solution.py:250
  47.3 1.6 %collective-permute-done.9.below = f32[12,512]{1,0:T(8,128)S(1)} collective-permute-done((f32[12,512]{1,0:T(8,128)S(1)}, f32[12,512]{1,0:T(8,128)S(1)}, u32[]{:S(2)}, u32[]{:S(2)}) %collective-permute-start.9) | collective-permute-done | bytes 24608 | tf_op jit(solution)/shard_map/ppermute | solution.py:250
  49.6 3.2 %collective-permute-done.11.refs_1_ = f32[8,512]{1,0:T(8,128)S(1)} collective-permute-done((f32[8,512]{1,0:T(8,128)S(1)}, f32[8,512]{1,0:T(8,128)S(1)}, u32[]{:S(2)}, u32[]{:S(2)}) %collective-permute-start.11) | collective-permute-done | bytes 16416 | tf_op jit(solution)/shard_map/ppermute | solution.py:228
  52.9 4.2 %collective-permute-start.12 = (f32[12,512]{1,0:T(8,128)S(1)}, f32[12,512]{1,0:T(8,128)S(1)}, u32[]{:S(2)}, u32[]{:S(2)}) collective-permute-start(f32[12,512]{1,0:T(8,128)S(1)} %get-tuple-element.79), channel_id=1, source_target_pairs={{0,4},{4,8},{8,12},{1,5},{5,9},{9,13},{2,6},{6,10},{10,14},{3,7},{... | collective-permute-start | bytes 73736 | tf_op jit(solution)/shard_map/ppermute | solution.py:250
  57.1 1.3 %collective-permute-start.13 = (f32[12,512]{1,0:T(8,128)S(1)}, f32[12,512]{1,0:T(8,128)S(1)}, u32[]{:S(2)}, u32[]{:S(2)}) collective-permute-start(f32[12,512]{1,0:T(8,128)S(1)} %get-tuple-element.80), channel_id=1, source_target_pairs={{4,0},{8,4},{12,8},{5,1},{9,5},{13,9},{6,2},{10,6},{14,10},{7,3},{... | collective-permute-start | bytes 73736 | tf_op jit(solution)/shard_map/ppermute | solution.py:251
  58.7 4.2 %collective-permute-done.13.above = f32[12,512]{1,0:T(8,128)S(1)} collective-permute-done((f32[12,512]{1,0:T(8,128)S(1)}, f32[12,512]{1,0:T(8,128)S(1)}, u32[]{:S(2)}, u32[]{:S(2)}) %collective-permute-start.13) | collective-permute-done | bytes 24608 | tf_op jit(solution)/shard_map/ppermute | solution.py:251
  63.8 3.1 %collective-permute-done.14.refs_1_ = f32[8,512]{1,0:T(8,128)S(1)} collective-permute-done((f32[8,512]{1,0:T(8,128)S(1)}, f32[8,512]{1,0:T(8,128)S(1)}, u32[]{:S(2)}, u32[]{:S(2)}) %collective-permute-start.14) | collective-permute-done | bytes 16416 | tf_op jit(solution)/shard_map/ppermute | solution.py:228
  66.9 1.9 %collective-permute-start.15 = (f32[12,512]{1,0:T(8,128)S(1)}, f32[12,512]{1,0:T(8,128)S(1)}, u32[]{:S(2)}, u32[]{:S(2)}) collective-permute-start(f32[12,512]{1,0:T(8,128)S(1)} %get-tuple-element.85), channel_id=1, source_target_pairs={{0,4},{4,8},{8,12},{1,5},{5,9},{9,13},{2,6},{6,10},{10,14},{3,7},{... | collective-permute-start | bytes 73736 | tf_op jit(solution)/shard_map/ppermute | solution.py:250
  68.9 1.3 %collective-permute-start.16 = (f32[12,512]{1,0:T(8,128)S(1)}, f32[12,512]{1,0:T(8,128)S(1)}, u32[]{:S(2)}, u32[]{:S(2)}) collective-permute-start(f32[12,512]{1,0:T(8,128)S(1)} %get-tuple-element.86), channel_id=1, source_target_pairs={{4,0},{8,4},{12,8},{5,1},{9,5},{13,9},{6,2},{10,6},{14,10},{7,3},{... | collective-permute-start | bytes 73736 | tf_op jit(solution)/shard_map/ppermute | solution.py:251
  70.7 4.3 %collective-permute-done.16.above = f32[12,512]{1,0:T(8,128)S(1)} collective-permute-done((f32[12,512]{1,0:T(8,128)S(1)}, f32[12,512]{1,0:T(8,128)S(1)}, u32[]{:S(2)}, u32[]{:S(2)}) %collective-permute-start.16) | collective-permute-done | bytes 24608 | tf_op jit(solution)/shard_map/ppermute | solution.py:251
  75.2 1.1 %collective-permute-start.17 = (f32[8,512]{1,0:T(8,128)S(1)}, f32[8,512]{1,0:T(8,128)S(1)}, u32[]{:S(2)}, u32[]{:S(2)}) collective-permute-start(f32[8,512]{1,0:T(8,128)S(1)} %get-tuple-element.88), channel_id=1, source_target_pairs={{0,2},{2,0},{1,3},{3,1},{4,6},{6,4},{5,7},{7,5},{8,10},{10,8},{9,1... | collective-permute-start | bytes 49160 | tf_op jit(solution)/shard_map/ppermute | solution.py:228
  76.3 2.7 %collective-permute-done.17.refs_1_ = f32[8,512]{1,0:T(8,128)S(1)} collective-permute-done((f32[8,512]{1,0:T(8,128)S(1)}, f32[8,512]{1,0:T(8,128)S(1)}, u32[]{:S(2)}, u32[]{:S(2)}) %collective-permute-start.17) | collective-permute-done | bytes 16416 | tf_op jit(solution)/shard_map/ppermute | solution.py:228
  79.1 3.0 %collective-permute-start.23 = (f32[8,256]{1,0:T(8,128)S(1)}, f32[8,256]{1,0:T(8,128)S(1)}, u32[]{:S(2)}, u32[]{:S(2)}) collective-permute-start(f32[8,256]{1,0:T(8,128)S(1)} %slice.12), channel_id=1, source_target_pairs={{0,2},{1,3},{4,6},{5,7},{8,10},{9,11},{12,14},{13,15},{16,18},{17,... | collective-permute-start | bytes 24584 | tf_op jit(solution)/shard_map/ppermute | solution.py:266
  83.9 3.4 %collective-permute-start.22 = (f32[13,16,128]{2,1,0:T(8,128)S(1)}, f32[13,16,128]{2,1,0:T(8,128)S(1)}, u32[]{:S(2)}, u32[]{:S(2)}) collective-permute-start(f32[13,16,128]{2,1,0:T(8,128)S(1)} %get-tuple-element.96), channel_id=1, source_target_pairs={{0,12},{4,0},{8,4},{12,8},{1,13},{5,1},{9,5},{13,9},{2,14},{6,2},{... | collective-permute-start | bytes 319496 | tf_op jit(solution)/shard_map/ppermute | solution.py:170
  87.3 2.5 %collective-permute-start.18 = (f32[12,512]{1,0:T(8,128)S(1)}, f32[12,512]{1,0:T(8,128)S(1)}, u32[]{:S(2)}, u32[]{:S(2)}) collective-permute-start(f32[12,512]{1,0:T(8,128)S(1)} %get-tuple-element.91), channel_id=1, source_target_pairs={{0,4},{4,8},{8,12},{1,5},{5,9},{9,13},{2,6},{6,10},{10,14},{3,7},{... | collective-permute-start | bytes 73736 | tf_op jit(solution)/shard_map/ppermute | solution.py:250
  89.7 1.3 %collective-permute-start.19 = (f32[12,512]{1,0:T(8,128)S(1)}, f32[12,512]{1,0:T(8,128)S(1)}, u32[]{:S(2)}, u32[]{:S(2)}) collective-permute-start(f32[12,512]{1,0:T(8,128)S(1)} %get-tuple-element.92), channel_id=1, source_target_pairs={{4,0},{8,4},{12,8},{5,1},{9,5},{13,9},{6,2},{10,6},{14,10},{7,3},{... | collective-permute-start | bytes 73736 | tf_op jit(solution)/shard_map/ppermute | solution.py:251
  91.8 3.8 %collective-permute-done.19.above = f32[12,512]{1,0:T(8,128)S(1)} collective-permute-done((f32[12,512]{1,0:T(8,128)S(1)}, f32[12,512]{1,0:T(8,128)S(1)}, u32[]{:S(2)}, u32[]{:S(2)}) %collective-permute-start.19) | collective-permute-done | bytes 24608 | tf_op jit(solution)/shard_map/ppermute | solution.py:251
  95.6 1.2 %shard_map.90 = f32[12,8,512]{2,1,0:T(8,128)} custom-call(f32[12,8,512]{2,1,0:T(8,128)S(1)} %get-tuple-element.90.lam, f32[12,512]{1,0:T(8,128)S(1)} %collective-permute-done.18.below, f32[12,512]{1,0:T(8,128)S(1)} %collective-permute-done.19.above, f32[12,8,512]{2,1,0:T(8,128)S(1)} %get-tuple-element.56.me, f32[12,8,512]{2,1,0:T(8,128)S(1)} %get-tuple-element.57.mw, ...), custom_call_target="tpu_custom_call" | custom-call | tf_op jit(solution)/shard_map/pallas_call | solution.py:16
  (51 shorter events, 9.0 us)
Async XLA Ops:
  0.6 4.0 %copy-start = (f32[2,12,8,512]{3,2,1,0:T(8,128)S(1)}, f32[2,12,8,512]{3,2,1,0:T(8,128)}, u32[]{:S(2)}) copy-start(f32[2,12,8,512]{3,2,1,0:T(8,128)} %courant.1) | copy-start | bytes 1179652
  1.7 6.0 %collective-permute-start = (f32[13,8,256]{2,1,0:T(8,128)S(1)}, f32[13,8,256]{2,1,0:T(8,128)S(1)}, u32[]{:S(2)}, u32[]{:S(2)}) collective-permute-start(f32[13,8,256]{2,1,0:T(8,128)S(1)} %get-tuple-element.100), channel_id=1, source_target_pairs={{0,2},{2,0},{1,3},{3,1},{4,6},{6,4},{5,7},{7,5},{8,10},{10,8},{9,1... | collective-permute-start | bytes 319496 | tf_op jit(solution)/shard_map/ppermute | solution.py:184
  4.7 5.8 %collective-permute-start.1 = (f32[12,512]{1,0:T(8,128)S(1)}, f32[12,512]{1,0:T(8,128)S(1)}, u32[]{:S(2)}, u32[]{:S(2)}) collective-permute-start(f32[12,512]{1,0:T(8,128)S(1)} %bitcast.22), channel_id=1, source_target_pairs={{4,0},{8,4},{12,8},{5,1},{9,5},{13,9},{6,2},{10,6},{14,10},{7,3},{... | collective-permute-start | bytes 73736 | tf_op jit(solution)/shard_map/ppermute | solution.py:207
  7.7 2.8 %copy-start.2 = (f32[1,12,8,512]{3,2,1,0:T(8,128)S(1)}, f32[1,12,8,512]{3,2,1,0:T(8,128)}, u32[]{:S(2)}) copy-start(f32[1,12,8,512]{3,2,1,0:T(8,128)} %param.6) | copy-start | bytes 589828
  10.7 4.0 %collective-permute-start.2 = (f32[2,8,512]{2,1,0:T(8,128)S(1)}, f32[2,8,512]{2,1,0:T(8,128)S(1)}, u32[]{:S(2)}, u32[]{:S(2)}) collective-permute-start(f32[2,8,512]{2,1,0:T(8,128)S(1)} %get-tuple-element.51), channel_id=1, source_target_pairs={{0,2},{2,0},{1,3},{3,1},{4,6},{6,4},{5,7},{7,5},{8,10},{10,8},{9,1... | collective-permute-start | bytes 98312 | tf_op jit(solution)/shard_map/ppermute | solution.py:228
  14.7 5.1 %collective-permute-start.3 = (f32[12,512]{1,0:T(8,128)S(1)}, f32[12,512]{1,0:T(8,128)S(1)}, u32[]{:S(2)}, u32[]{:S(2)}) collective-permute-start(f32[12,512]{1,0:T(8,128)S(1)} %get-tuple-element.54), channel_id=1, source_target_pairs={{0,4},{4,8},{8,12},{1,5},{5,9},{9,13},{2,6},{6,10},{10,14},{3,7},{... | collective-permute-start | bytes 73736 | tf_op jit(solution)/shard_map/ppermute | solution.py:250
  18.2 5.8 %collective-permute-start.4 = (f32[12,512]{1,0:T(8,128)S(1)}, f32[12,512]{1,0:T(8,128)S(1)}, u32[]{:S(2)}, u32[]{:S(2)}) collective-permute-start(f32[12,512]{1,0:T(8,128)S(1)} %get-tuple-element.55), channel_id=1, source_target_pairs={{4,0},{8,4},{12,8},{5,1},{9,5},{13,9},{6,2},{10,6},{14,10},{7,3},{... | collective-permute-start | bytes 73736 | tf_op jit(solution)/shard_map/ppermute | solution.py:251
  24.2 3.8 %collective-permute-start.5 = (f32[8,512]{1,0:T(8,128)S(1)}, f32[8,512]{1,0:T(8,128)S(1)}, u32[]{:S(2)}, u32[]{:S(2)}) collective-permute-start(f32[8,512]{1,0:T(8,128)S(1)} %get-tuple-element.63), channel_id=1, source_target_pairs={{0,2},{2,0},{1,3},{3,1},{4,6},{6,4},{5,7},{7,5},{8,10},{10,8},{9,1... | collective-permute-start | bytes 49160 | tf_op jit(solution)/shard_map/ppermute | solution.py:228
  28.1 5.1 %collective-permute-start.6 = (f32[12,512]{1,0:T(8,128)S(1)}, f32[12,512]{1,0:T(8,128)S(1)}, u32[]{:S(2)}, u32[]{:S(2)}) collective-permute-start(f32[12,512]{1,0:T(8,128)S(1)} %get-tuple-element.67), channel_id=1, source_target_pairs={{0,4},{4,8},{8,12},{1,5},{5,9},{9,13},{2,6},{6,10},{10,14},{3,7},{... | collective-permute-start | bytes 73736 | tf_op jit(solution)/shard_map/ppermute | solution.py:250
  31.5 5.8 %collective-permute-start.7 = (f32[12,512]{1,0:T(8,128)S(1)}, f32[12,512]{1,0:T(8,128)S(1)}, u32[]{:S(2)}, u32[]{:S(2)}) collective-permute-start(f32[12,512]{1,0:T(8,128)S(1)} %get-tuple-element.68), channel_id=1, source_target_pairs={{4,0},{8,4},{12,8},{5,1},{9,5},{13,9},{6,2},{10,6},{14,10},{7,3},{... | collective-permute-start | bytes 73736 | tf_op jit(solution)/shard_map/ppermute | solution.py:251
  37.5 3.8 %collective-permute-start.8 = (f32[8,512]{1,0:T(8,128)S(1)}, f32[8,512]{1,0:T(8,128)S(1)}, u32[]{:S(2)}, u32[]{:S(2)}) collective-permute-start(f32[8,512]{1,0:T(8,128)S(1)} %get-tuple-element.70), channel_id=1, source_target_pairs={{0,2},{2,0},{1,3},{3,1},{4,6},{6,4},{5,7},{7,5},{8,10},{10,8},{9,1... | collective-permute-start | bytes 49160 | tf_op jit(solution)/shard_map/ppermute | solution.py:228
  41.4 5.9 %collective-permute-start.10 = (f32[12,512]{1,0:T(8,128)S(1)}, f32[12,512]{1,0:T(8,128)S(1)}, u32[]{:S(2)}, u32[]{:S(2)}) collective-permute-start(f32[12,512]{1,0:T(8,128)S(1)} %get-tuple-element.74), channel_id=1, source_target_pairs={{4,0},{8,4},{12,8},{5,1},{9,5},{13,9},{6,2},{10,6},{14,10},{7,3},{... | collective-permute-start | bytes 73736 | tf_op jit(solution)/shard_map/ppermute | solution.py:251
  42.7 6.1 %collective-permute-start.9 = (f32[12,512]{1,0:T(8,128)S(1)}, f32[12,512]{1,0:T(8,128)S(1)}, u32[]{:S(2)}, u32[]{:S(2)}) collective-permute-start(f32[12,512]{1,0:T(8,128)S(1)} %get-tuple-element.73), channel_id=1, source_target_pairs={{0,4},{4,8},{8,12},{1,5},{5,9},{9,13},{2,6},{6,10},{10,14},{3,7},{... | collective-permute-start | bytes 73736 | tf_op jit(solution)/shard_map/ppermute | solution.py:250
  49.0 3.8 %collective-permute-start.11 = (f32[8,512]{1,0:T(8,128)S(1)}, f32[8,512]{1,0:T(8,128)S(1)}, u32[]{:S(2)}, u32[]{:S(2)}) collective-permute-start(f32[8,512]{1,0:T(8,128)S(1)} %get-tuple-element.76), channel_id=1, source_target_pairs={{0,2},{2,0},{1,3},{3,1},{4,6},{6,4},{5,7},{7,5},{8,10},{10,8},{9,1... | collective-permute-start | bytes 49160 | tf_op jit(solution)/shard_map/ppermute | solution.py:228
  52.9 5.8 %collective-permute-start.12 = (f32[12,512]{1,0:T(8,128)S(1)}, f32[12,512]{1,0:T(8,128)S(1)}, u32[]{:S(2)}, u32[]{:S(2)}) collective-permute-start(f32[12,512]{1,0:T(8,128)S(1)} %get-tuple-element.79), channel_id=1, source_target_pairs={{0,4},{4,8},{8,12},{1,5},{5,9},{9,13},{2,6},{6,10},{10,14},{3,7},{... | collective-permute-start | bytes 73736 | tf_op jit(solution)/shard_map/ppermute | solution.py:250
  57.1 5.8 %collective-permute-start.13 = (f32[12,512]{1,0:T(8,128)S(1)}, f32[12,512]{1,0:T(8,128)S(1)}, u32[]{:S(2)}, u32[]{:S(2)}) collective-permute-start(f32[12,512]{1,0:T(8,128)S(1)} %get-tuple-element.80), channel_id=1, source_target_pairs={{4,0},{8,4},{12,8},{5,1},{9,5},{13,9},{6,2},{10,6},{14,10},{7,3},{... | collective-permute-start | bytes 73736 | tf_op jit(solution)/shard_map/ppermute | solution.py:251
  63.1 3.8 %collective-permute-start.14 = (f32[8,512]{1,0:T(8,128)S(1)}, f32[8,512]{1,0:T(8,128)S(1)}, u32[]{:S(2)}, u32[]{:S(2)}) collective-permute-start(f32[8,512]{1,0:T(8,128)S(1)} %get-tuple-element.82), channel_id=1, source_target_pairs={{0,2},{2,0},{1,3},{3,1},{4,6},{6,4},{5,7},{7,5},{8,10},{10,8},{9,1... | collective-permute-start | bytes 49160 | tf_op jit(solution)/shard_map/ppermute | solution.py:228
  66.9 3.7 %collective-permute-start.15 = (f32[12,512]{1,0:T(8,128)S(1)}, f32[12,512]{1,0:T(8,128)S(1)}, u32[]{:S(2)}, u32[]{:S(2)}) collective-permute-start(f32[12,512]{1,0:T(8,128)S(1)} %get-tuple-element.85), channel_id=1, source_target_pairs={{0,4},{4,8},{8,12},{1,5},{5,9},{9,13},{2,6},{6,10},{10,14},{3,7},{... | collective-permute-start | bytes 73736 | tf_op jit(solution)/shard_map/ppermute | solution.py:250
  68.9 6.2 %collective-permute-start.16 = (f32[12,512]{1,0:T(8,128)S(1)}, f32[12,512]{1,0:T(8,128)S(1)}, u32[]{:S(2)}, u32[]{:S(2)}) collective-permute-start(f32[12,512]{1,0:T(8,128)S(1)} %get-tuple-element.86), channel_id=1, source_target_pairs={{4,0},{8,4},{12,8},{5,1},{9,5},{13,9},{6,2},{10,6},{14,10},{7,3},{... | collective-permute-start | bytes 73736 | tf_op jit(solution)/shard_map/ppermute | solution.py:251
  75.2 7.6 %copy-start.1 = (f32[1,12,64,128]{3,2,1,0:T(8,128)S(1)}, f32[1,12,64,128]{3,2,1,0:T(8,128)}, u32[]{:S(2)}) copy-start(f32[1,12,64,128]{3,2,1,0:T(8,128)} %param.9) | copy-start | bytes 1179652
  75.2 3.8 %collective-permute-start.17 = (f32[8,512]{1,0:T(8,128)S(1)}, f32[8,512]{1,0:T(8,128)S(1)}, u32[]{:S(2)}, u32[]{:S(2)}) collective-permute-start(f32[8,512]{1,0:T(8,128)S(1)} %get-tuple-element.88), channel_id=1, source_target_pairs={{0,2},{2,0},{1,3},{3,1},{4,6},{6,4},{5,7},{7,5},{8,10},{10,8},{9,1... | collective-permute-start | bytes 49160 | tf_op jit(solution)/shard_map/ppermute | solution.py:228
  79.1 3.0 %copy-start.4 = (s32[64]{0:T(128)S(1)}, s32[64]{0:T(128)}, u32[]{:S(2)}) copy-start(s32[64]{0:T(128)} %param.11) | copy-start | bytes 772
  79.1 10.6 %collective-permute-start.23 = (f32[8,256]{1,0:T(8,128)S(1)}, f32[8,256]{1,0:T(8,128)S(1)}, u32[]{:S(2)}, u32[]{:S(2)}) collective-permute-start(f32[8,256]{1,0:T(8,128)S(1)} %slice.12), channel_id=1, source_target_pairs={{0,2},{1,3},{4,6},{5,7},{8,10},{9,11},{12,14},{13,15},{16,18},{17,... | collective-permute-start | bytes 24584 | tf_op jit(solution)/shard_map/ppermute | solution.py:266
  82.1 0.7 copy-start.3
  83.4 8.2 %collective-permute-start.20 = (f32[13,16,128]{2,1,0:T(8,128)S(1)}, f32[13,16,128]{2,1,0:T(8,128)S(1)}, u32[]{:S(2)}, u32[]{:S(2)}) collective-permute-start(f32[13,16,128]{2,1,0:T(8,128)S(1)} %get-tuple-element.94), channel_id=1, source_target_pairs={{0,4},{4,8},{8,12},{12,0},{1,5},{5,9},{9,13},{13,1},{2,6},{6,10},{... | collective-permute-start | bytes 319496 | tf_op jit(solution)/shard_map/ppermute | solution.py:170
  83.9 7.9 %collective-permute-start.21 = (f32[13,16,128]{2,1,0:T(8,128)S(1)}, f32[13,16,128]{2,1,0:T(8,128)S(1)}, u32[]{:S(2)}, u32[]{:S(2)}) collective-permute-start(f32[13,16,128]{2,1,0:T(8,128)S(1)} %get-tuple-element.95), channel_id=1, source_target_pairs={{0,8},{4,12},{8,0},{12,4},{1,9},{5,13},{9,1},{13,5},{2,10},{6,14},... | collective-permute-start | bytes 319496 | tf_op jit(solution)/shard_map/ppermute | solution.py:170
  83.9 7.9 %collective-permute-start.22 = (f32[13,16,128]{2,1,0:T(8,128)S(1)}, f32[13,16,128]{2,1,0:T(8,128)S(1)}, u32[]{:S(2)}, u32[]{:S(2)}) collective-permute-start(f32[13,16,128]{2,1,0:T(8,128)S(1)} %get-tuple-element.96), channel_id=1, source_target_pairs={{0,12},{4,0},{8,4},{12,8},{1,13},{5,1},{9,5},{13,9},{2,14},{6,2},{... | collective-permute-start | bytes 319496 | tf_op jit(solution)/shard_map/ppermute | solution.py:170
  87.3 4.5 %collective-permute-start.18 = (f32[12,512]{1,0:T(8,128)S(1)}, f32[12,512]{1,0:T(8,128)S(1)}, u32[]{:S(2)}, u32[]{:S(2)}) collective-permute-start(f32[12,512]{1,0:T(8,128)S(1)} %get-tuple-element.91), channel_id=1, source_target_pairs={{0,4},{4,8},{8,12},{1,5},{5,9},{9,13},{2,6},{6,10},{10,14},{3,7},{... | collective-permute-start | bytes 73736 | tf_op jit(solution)/shard_map/ppermute | solution.py:250
  89.7 5.8 %collective-permute-start.19 = (f32[12,512]{1,0:T(8,128)S(1)}, f32[12,512]{1,0:T(8,128)S(1)}, u32[]{:S(2)}, u32[]{:S(2)}) collective-permute-start(f32[12,512]{1,0:T(8,128)S(1)} %get-tuple-element.92), channel_id=1, source_target_pairs={{4,0},{8,4},{12,8},{5,1},{9,5},{13,9},{6,2},{10,6},{14,10},{7,3},{... | collective-permute-start | bytes 73736 | tf_op jit(solution)/shard_map/ppermute | solution.py:251
where the time goes:
time: 97.2 us; the launch traced here: 96.8 us
  waiting for transfers between devices  47.4 us (49%)
  starting transfers between devices  42.8 us (44%)
  Pallas kernels  3.08 us (3%)
  local copies, waits for them, and re-layouts  1.8 us (2%)
  between operations  0.98 us (1%)
    ppermute x6, waiting for transfers between devices, local(): above = lax.ppermute(south, 'lat', southward)  20.8 us
    ppermute x6, starting transfers between devices, local(): below = lax.ppermute(north, 'lat', northward)  20.1 us
    ppermute x6, waiting for transfers between devices, local(): met = lax.ppermute(ends, 'lev', meet)  19.2 us
    ppermute x6, starting transfers between devices, local(): above = lax.ppermute(south, 'lat', southward)  7.75 us
    ppermute x3, starting transfers between devices, route_tiles(): lax.ppermute(outs[s], 'lat', [(b, (b + s) % regions) for b in range(regio...  3.85 us
    ppermute x6, starting transfers between devices, local(): met = lax.ppermute(ends, 'lev', meet)  3.81 us
    pallas_call x14, Pallas kernels, call(): pl.pallas_call(body, out_shape=[jax.ShapeDtypeStruct(shape, F32) for shap...  3.08 us
    ppermute x1, starting transfers between devices, diffusion_window(): lax.ppermute(part, 'lev', [(p, (p + shift) % devices) for p in range(devi...  3 us
  transfers between devices with their start and end apart: 24, of which 19 were waited for; matrix products, arithmetic and copies ran while one was open for 1% of the time, Pallas kernels for 1%

commit v1 on v0

--- a/solution.py
+++ b/solution.py
@@ -30,12 +30,31 @@
     return lax.axis_index("lev") < devices // 2
 
 
-def prepare_body(devices, field, window, courant, face_north, gain_in, y_in, *outs):
+def even_band():
+    return lax.rem(lax.axis_index("lat"), 2) == 0
+
+
+def band_swaps(bands, first):
+    swaps = []
+    for b in range(bands):
+        partner = b + 1 if (b - first) % 2 == 0 else b - 1
+        swaps.append((b, partner if 0 <= partner < bands else b))
+    return swaps
+
+
+def partner_of(band, shift, bands):
+    if bands & (bands - 1) == 0:
+        return band ^ shift
+    return (band + shift) % bands
+
+
+def prepare_body(devices, bands, field, window, courant, face_north, gain_in, y_in, *outs):
     r_out, a_out, g_out, me_out, mw_out, ze_out, zw_out, y_out, ends_out = outs
     count, rows, width = field.shape
     upper = upper_half(devices)
     row = lax.broadcasted_iota(jnp.int32, (rows, width), 0)
     first_row = (row == 0) & (lax.axis_index("lat") == 0)
+    last_row = (row == rows - 1) & (lax.axis_index("lat") == bands - 1)
     gain, y = gain_in[...], y_in[...]
     for i in range(count):
         level = order(i, count, upper)
@@ -50,7 +69,7 @@
         south = courant[1, level]
         north = pltpu.roll(south, rows - 1, 0)
         north = jnp.where(row == rows - 1, face_north[pl.ds(level, 1), :], north)
-        me_out[i] = jnp.maximum(north, 0.0)
+        me_out[i] = jnp.where(last_row, 0.0, jnp.maximum(north, 0.0))
         mw_out[i] = jnp.where(first_row, 0.0, jnp.minimum(south, 0.0))
         west = courant[0, level]
         ze_out[i] = jnp.maximum(pltpu.roll(west, width - 1, 1), 0.0)
@@ -61,9 +80,9 @@
 
 def back_body(devices, first, *refs):
     if first:
-        y, other, g, lam, south, north, flux, scale_out = refs
+        y, other, g, lam, edge_a, edge_b, flux, scale_out = refs
     else:
-        y, other, g, scale, flux_in, lam, south, north, flux = refs
+        y, other, g, scale, flux_in, lam, edge_a, edge_b, flux = refs
     count, rows, _ = y.shape
     last = count - 1
     if first:
@@ -76,36 +95,40 @@
         scale = scale[...]
         met = other[...]
     w = (y[last] + g[last] * met) * scale
+    even = even_band()
     for i in range(last, -1, -1):
         if i < last:
             w = y[i] + g[i] * w
         lam[i] = w
-        south[pl.ds(i, 1), :] = w[0:1, :]
-        north[pl.ds(i, 1), :] = w[rows - 1 : rows, :]
+        south, north = w[0:1, :], w[rows - 1 : rows, :]
+        edge_a[pl.ds(i, 1), :] = jnp.where(even, north, south)
+        edge_b[pl.ds(i, 1), :] = jnp.where(even, south, north)
     flux[...] = w if first else flux_in[...] + w
 
 
-def advect(i, lam, below, above, me, mw, ze, zw):
+def advect(i, lam, edge_a, edge_b, me, mw, ze, zw):
     _, rows, width = lam.shape
     row = lax.broadcasted_iota(jnp.int32, (rows, width), 0)
     v = lam[i]
-    up = jnp.where(row == rows - 1, above[pl.ds(i, 1), :], pltpu.roll(v, rows - 1, 0))
-    down = jnp.where(row == 0, below[pl.ds(i, 1), :], pltpu.roll(v, 1, 0))
+    even = even_band()
+    a, b = edge_a[pl.ds(i, 1), :], edge_b[pl.ds(i, 1), :]
+    up = jnp.where(row == rows - 1, jnp.where(even, a, b), pltpu.roll(v, rows - 1, 0))
+    down = jnp.where(row == 0, jnp.where(even, b, a), pltpu.roll(v, 1, 0))
     v = v + me[i] * (up - v) + mw[i] * (v - down)
     east = pltpu.roll(v, width - 1, 1)
     west = pltpu.roll(v, 1, 1)
     return v + ze[i] * (east - v) + zw[i] * (v - west)
 
 
-def forward_body(lam, below, above, me, mw, ze, zw, r, a, y_in, y_out, end_out):
+def forward_body(lam, edge_a, edge_b, me, mw, ze, zw, r, a, y_in, y_out, end_out):
     y = y_in[...]
     for i in range(lam.shape[0]):
-        y = advect(i, lam, below, above, me, mw, ze, zw) * r[i] + a[i] * y
+        y = advect(i, lam, edge_a, edge_b, me, mw, ze, zw) * r[i] + a[i] * y
         y_out[i] = y
     end_out[...] = y
 
 
-def finish_body(devices, lam, below, above, me, mw, ze, zw, *rest):
+def finish_body(devices, lam, edge_a, edge_b, me, mw, ze, zw, *rest):
     buckets, out = rest[:-1], rest[-1]
     count, rows, width = lam.shape
     upper = upper_half(devices)
@@ -118,7 +141,7 @@
     hits = hits.T[: rows * blocks]
     for i in range(count):
         level = order(i, count, upper)
-        v = advect(i, lam, below, above, me, mw, ze, zw)
+        v = advect(i, lam, edge_a, edge_b, me, mw, ze, zw)
         values = jnp.concatenate([bucket[level] for bucket in buckets], axis=0)
         added = lax.dot_general(
             hits, values, (((1,), (0,)), ((), ())), precision=lax.Precision.HIGHEST, preferred_element_type=F32
@@ -139,7 +162,7 @@
     slot = lax.broadcasted_iota(jnp.int32, (capacity, tiles), 0)
     cells = jnp.broadcast_to(cell_column[...].astype(F32), (tiles, tile))
     picks = [
-        jnp.where((slot == rank) & (region_row[...] == lax.rem(band + s, regions)), 1.0, 0.0) for s in range(regions)
+        jnp.where((slot == rank) & (region_row[...] == partner_of(band, s, regions)), 1.0, 0.0) for s in range(regions)
     ]
     picks = jnp.concatenate(picks, axis=0)
     for level in range(count + 1):
@@ -167,7 +190,7 @@
     )
     got = [outs[0]]
     for s in range(1, regions):
-        got.append(lax.ppermute(outs[s], "lat", [(b, (b + s) % regions) for b in range(regions)]))
+        got.append(lax.ppermute(outs[s], "lat", [(b, partner_of(b, s, regions)) for b in range(regions)]))
     return got
 
 
@@ -199,19 +222,18 @@
     inward = [(p, p + 1) for p in range(half - 1)] + [(p, p - 1) for p in range(half + 1, devices)]
     outward = [(b, a) for a, b in inward]
     meet = [(half - 1, half), (half, half - 1)]
-    northward = [(b, b + 1) for b in range(bands - 1)]
-    southward = [(b + 1, b) for b in range(bands - 1)]
+    swaps_a, swaps_b = band_swaps(bands, 0), band_swaps(bands, 1)
 
     buckets = route_tiles(tile_values[0], tile_region, tile_cell)
     window = diffusion_window(diffusion, count)
-    face_north = lax.ppermute(courant[1, :, 0, :], "lat", southward)
+    face_north = lax.ppermute(courant[1, :, 0, :], "lat", [(b, (b - 1) % bands) for b in range(bands)])
 
     whole, plane, edge = (count, rows, width), (rows, width), (count, width)
     zero = jnp.zeros(plane, F32)
     gain_in, y_in = zero, zero
     for turn in range(half):
         r, a, g, me, mw, ze, zw, y, ends = call(
-            functools.partial(prepare_body, devices),
+            functools.partial(prepare_body, devices, bands),
             [whole] * 8 + [(2,) + plane],
             field,
             window,
@@ -228,11 +250,11 @@
         met = lax.ppermute(ends, "lev", meet)
         for turn in range(half):
             if step == 0:
-                lam, south, north, new_flux, scale = call(
+                lam, edge_a, edge_b, new_flux, scale = call(
                     functools.partial(back_body, devices, True), [whole, edge, edge, plane, plane], y, met, g
                 )
             else:
-                lam, south, north, new_flux = call(
+                lam, edge_a, edge_b, new_flux = call(
                     functools.partial(back_body, devices, False),
                     [whole, edge, edge, plane],
                     y,
@@ -247,9 +269,9 @@
                     passed = jnp.stack([passed, jnp.zeros_like(passed)])
                 met = jnp.where(innermost, met, passed)
         flux = new_flux
-        below = lax.ppermute(north, "lat", northward)
-        above = lax.ppermute(south, "lat", southward)
-        args = (lam, below, above, me, mw, ze, zw)
+        edge_a = lax.ppermute(edge_a, "lat", swaps_a)
+        edge_b = lax.ppermute(edge_b, "lat", swaps_b)
+        args = (lam, edge_a, edge_b, me, mw, ze, zw)
         if step == STEPS - 1:
             (out,) = call(functools.partial(finish_body, devices), [whole], *args, *buckets)
             break
@@ -263,7 +285,7 @@
     chunk = width // devices
     share = flux[:, :chunk]
     for p in range(1, devices):
-        sent = lax.ppermute(flux[:, p * chunk : (p + 1) * chunk], "lev", [(0, p)])
+        sent = lax.ppermute(flux[:, p * chunk : (p + 1) * chunk], "lev", [(0, p), (p, 0)])
         share = jnp.where(at == p, sent, share)
     return out[None], share[None]
 

time: 97.2 us -> 81.4 us (0.84)
  waiting for transfers between devices: 47.4 us -> 33 us
  starting transfers between devices: 42.8 us -> 41.4 us
    ppermute x17, waiting for transfers between devices: 26.6 us -> 13.5 us  [the longest x6 8.72 us: local(): edge_a = lax.ppermute(edge_a, 'lat', swaps_a)]
    ppermute x1, waiting for transfers between devices: 1.6 us -> 0.01 us  [diffusion_window(): lax.ppermute(part, 'lev', [(p, (p + shift) % devices) for p in range(devi...]
    ppermute x17, starting transfers between devices: 36 us -> 34.9 us  [the longest x6 20.1 us: local(): edge_a = lax.ppermute(edge_a, 'lat', swaps_a)]
  transfers between devices with their start and end apart: 24 -> 24, of which waited for: 19 -> 14; matrix products, arithmetic and copies ran while one was open for 1% -> 1% of each run, Pallas kernels for 1% -> 1%
where the time goes in v1:
time: 81.4 us; the launch traced here: 81.1 us
  starting transfers between devices  41.4 us (51%)
  waiting for transfers between devices  33 us (41%)
  Pallas kernels  3.29 us (4%)
  local copies, waits for them, and re-layouts  1.95 us (2%)
  between operations  0.85 us (1%)
    ppermute x6, starting transfers between devices, local(): edge_a = lax.ppermute(edge_a, 'lat', swaps_a)  20.1 us
    ppermute x6, waiting for transfers between devices, local(): met = lax.ppermute(ends, 'lev', meet)  19.5 us
    ppermute x6, waiting for transfers between devices, local(): edge_a = lax.ppermute(edge_a, 'lat', swaps_a)  8.72 us
    ppermute x3, starting transfers between devices, route_tiles(): lax.ppermute(outs[s], 'lat', [(b, partner_of(b, s, regions)) for b in ran...  6.7 us
    ppermute x6, starting transfers between devices, local(): edge_b = lax.ppermute(edge_b, 'lat', swaps_b)  3.92 us
    ppermute x1, starting transfers between devices, local(): lax.ppermute(courant[1, :, 0, :], 'lat', [(b, (b - 1) % bands) for b in r...  3.65 us
    ppermute x6, starting transfers between devices, local(): met = lax.ppermute(ends, 'lev', meet)  3.49 us
    pallas_call x14, Pallas kernels, call(): pl.pallas_call(body, out_shape=[jax.ShapeDtypeStruct(shape, F32) for shap...  3.29 us
  transfers between devices with their start and end apart: 24, of which 14 were waited for; matrix products, arithmetic and copies ran while one was open for 1% of the time, Pallas kernels for 1%

profile of v1, /device:TPU:0, one launch (start us, length us, event | category | flops | bytes accessed | tf_op | source)
XLA Modules:
  0.0 81.1 jit_solution(11184725450681616317)
XLA Ops:
  0.7 1.0 %pad_dynamic-slice_fusion.4 = (f32[13,8,256]{2,1,0:T(8,128)S(1)}, f32[1,13,8,256]{3,2,1,0:T(8,128)S(1)}) fusion(s32[]{:T(128)S(6)} %select_n.32, f32[23,8,256]{2,1,0:T(8,128)} %param.8, s32[]{:T(128)S(6)} %select_n.31), kind=kLoop, calls=%fused_computation.5 | loop fusion | bytes 401416 | tf_op jit(solution)/shard_map/dynamic_slice | solution.py:205
  1.7 3.0 %collective-permute-start = (f32[13,8,256]{2,1,0:T(8,128)S(1)}, f32[13,8,256]{2,1,0:T(8,128)S(1)}, u32[]{:S(2)}, u32[]{:S(2)}) collective-permute-start(f32[13,8,256]{2,1,0:T(8,128)S(1)} %get-tuple-element.100), channel_id=1, source_target_pairs={{0,2},{2,0},{1,3},{3,1},{4,6},{6,4},{5,7},{7,5},{8,10},{10,8},{9,1... | collective-permute-start | bytes 319496 | tf_op jit(solution)/shard_map/ppermute | solution.py:207
  4.7 3.7 %collective-permute-start.1 = (f32[12,512]{1,0:T(8,128)S(1)}, f32[12,512]{1,0:T(8,128)S(1)}, u32[]{:S(2)}, u32[]{:S(2)}) collective-permute-start(f32[12,512]{1,0:T(8,128)S(1)} %bitcast.22), channel_id=1, source_target_pairs={{0,12},{4,0},{8,4},{12,8},{1,13},{5,1},{9,5},{13,9},{2,14},{6,2},{... | collective-permute-start | bytes 73736 | tf_op jit(solution)/shard_map/ppermute | solution.py:229
  8.5 1.5 %collective-permute-done.1.face_north = f32[12,512]{1,0:T(8,128)S(1)} collective-permute-done((f32[12,512]{1,0:T(8,128)S(1)}, f32[12,512]{1,0:T(8,128)S(1)}, u32[]{:S(2)}, u32[]{:S(2)}) %collective-permute-start.1) | collective-permute-done | bytes 24608 | tf_op jit(solution)/shard_map/ppermute | solution.py:229
  10.1 0.6 collective-permute-start.2
  10.7 3.4 %collective-permute-done.2.refs_1_ = f32[2,8,512]{2,1,0:T(8,128)S(1)} collective-permute-done((f32[2,8,512]{2,1,0:T(8,128)S(1)}, f32[2,8,512]{2,1,0:T(8,128)S(1)}, u32[]{:S(2)}, u32[]{:S(2)}) %collective-permute-start.2) | collective-permute-done | bytes 32800 | tf_op jit(solution)/shard_map/ppermute | solution.py:250
  14.7 0.7 collective-permute-start.4
  15.4 2.8 %collective-permute-done.3.edge_a = f32[12,512]{1,0:T(8,128)S(1)} collective-permute-done((f32[12,512]{1,0:T(8,128)S(1)}, f32[12,512]{1,0:T(8,128)S(1)}, u32[]{:S(2)}, u32[]{:S(2)}) %collective-permute-start.3) | collective-permute-done | bytes 24608 | tf_op jit(solution)/shard_map/ppermute | solution.py:272
  19.0 3.2 %collective-permute-done.5.refs_1_ = f32[8,512]{1,0:T(8,128)S(1)} collective-permute-done((f32[8,512]{1,0:T(8,128)S(1)}, f32[8,512]{1,0:T(8,128)S(1)}, u32[]{:S(2)}, u32[]{:S(2)}) %collective-permute-start.5) | collective-permute-done | bytes 16416 | tf_op jit(solution)/shard_map/ppermute | solution.py:250
  22.2 5.2 %collective-permute-start.6 = (f32[12,512]{1,0:T(8,128)S(1)}, f32[12,512]{1,0:T(8,128)S(1)}, u32[]{:S(2)}, u32[]{:S(2)}) collective-permute-start(f32[12,512]{1,0:T(8,128)S(1)} %get-tuple-element.67), channel_id=1, source_target_pairs={{0,4},{4,0},{8,12},{12,8},{1,5},{5,1},{9,13},{13,9},{2,6},{6,2},{1... | collective-permute-start | bytes 73736 | tf_op jit(solution)/shard_map/ppermute | solution.py:272
  27.4 0.7 collective-permute-start.7
  28.1 1.2 %collective-permute-done.6.edge_a = f32[12,512]{1,0:T(8,128)S(1)} collective-permute-done((f32[12,512]{1,0:T(8,128)S(1)}, f32[12,512]{1,0:T(8,128)S(1)}, u32[]{:S(2)}, u32[]{:S(2)}) %collective-permute-start.6) | collective-permute-done | bytes 24608 | tf_op jit(solution)/shard_map/ppermute | solution.py:272
  30.1 3.2 %collective-permute-done.8.refs_1_ = f32[8,512]{1,0:T(8,128)S(1)} collective-permute-done((f32[8,512]{1,0:T(8,128)S(1)}, f32[8,512]{1,0:T(8,128)S(1)}, u32[]{:S(2)}, u32[]{:S(2)}) %collective-permute-start.8) | collective-permute-done | bytes 16416 | tf_op jit(solution)/shard_map/ppermute | solution.py:250
  33.4 0.7 collective-permute-start.10
  34.1 7.2 %collective-permute-start.9 = (f32[12,512]{1,0:T(8,128)S(1)}, f32[12,512]{1,0:T(8,128)S(1)}, u32[]{:S(2)}, u32[]{:S(2)}) collective-permute-start(f32[12,512]{1,0:T(8,128)S(1)} %get-tuple-element.73), channel_id=1, source_target_pairs={{0,4},{4,0},{8,12},{12,8},{1,5},{5,1},{9,13},{13,9},{2,6},{6,2},{1... | collective-permute-start | bytes 73736 | tf_op jit(solution)/shard_map/ppermute | solution.py:272
  41.3 1.9 %collective-permute-done.9.edge_a = f32[12,512]{1,0:T(8,128)S(1)} collective-permute-done((f32[12,512]{1,0:T(8,128)S(1)}, f32[12,512]{1,0:T(8,128)S(1)}, u32[]{:S(2)}, u32[]{:S(2)}) %collective-permute-start.9) | collective-permute-done | bytes 24608 | tf_op jit(solution)/shard_map/ppermute | solution.py:272
  44.0 3.2 %collective-permute-done.11.refs_1_ = f32[8,512]{1,0:T(8,128)S(1)} collective-permute-done((f32[8,512]{1,0:T(8,128)S(1)}, f32[8,512]{1,0:T(8,128)S(1)}, u32[]{:S(2)}, u32[]{:S(2)}) %collective-permute-start.11) | collective-permute-done | bytes 16416 | tf_op jit(solution)/shard_map/ppermute | solution.py:250
  47.3 2.1 %collective-permute-start.12 = (f32[12,512]{1,0:T(8,128)S(1)}, f32[12,512]{1,0:T(8,128)S(1)}, u32[]{:S(2)}, u32[]{:S(2)}) collective-permute-start(f32[12,512]{1,0:T(8,128)S(1)} %get-tuple-element.79), channel_id=1, source_target_pairs={{0,4},{4,0},{8,12},{12,8},{1,5},{5,1},{9,13},{13,9},{2,6},{6,2},{1... | collective-permute-start | bytes 73736 | tf_op jit(solution)/shard_map/ppermute | solution.py:272
  49.3 0.7 collective-permute-start.13
  50.0 1.2 %collective-permute-done.12.edge_a = f32[12,512]{1,0:T(8,128)S(1)} collective-permute-done((f32[12,512]{1,0:T(8,128)S(1)}, f32[12,512]{1,0:T(8,128)S(1)}, u32[]{:S(2)}, u32[]{:S(2)}) %collective-permute-start.12) | collective-permute-done | bytes 24608 | tf_op jit(solution)/shard_map/ppermute | solution.py:272
  52.0 3.2 %collective-permute-done.14.refs_1_ = f32[8,512]{1,0:T(8,128)S(1)} collective-permute-done((f32[8,512]{1,0:T(8,128)S(1)}, f32[8,512]{1,0:T(8,128)S(1)}, u32[]{:S(2)}, u32[]{:S(2)}) %collective-permute-start.14) | collective-permute-done | bytes 16416 | tf_op jit(solution)/shard_map/ppermute | solution.py:250
  55.3 4.0 %collective-permute-start.15 = (f32[12,512]{1,0:T(8,128)S(1)}, f32[12,512]{1,0:T(8,128)S(1)}, u32[]{:S(2)}, u32[]{:S(2)}) collective-permute-start(f32[12,512]{1,0:T(8,128)S(1)} %get-tuple-element.85), channel_id=1, source_target_pairs={{0,4},{4,0},{8,12},{12,8},{1,5},{5,1},{9,13},{13,9},{2,6},{6,2},{1... | collective-permute-start | bytes 73736 | tf_op jit(solution)/shard_map/ppermute | solution.py:272
  59.3 0.7 collective-permute-start.16
  60.0 1.4 %collective-permute-done.15.edge_a = f32[12,512]{1,0:T(8,128)S(1)} collective-permute-done((f32[12,512]{1,0:T(8,128)S(1)}, f32[12,512]{1,0:T(8,128)S(1)}, u32[]{:S(2)}, u32[]{:S(2)}) %collective-permute-start.15) | collective-permute-done | bytes 24608 | tf_op jit(solution)/shard_map/ppermute | solution.py:272
  62.0 3.3 %collective-permute-done.17.refs_1_ = f32[8,512]{1,0:T(8,128)S(1)} collective-permute-done((f32[8,512]{1,0:T(8,128)S(1)}, f32[8,512]{1,0:T(8,128)S(1)}, u32[]{:S(2)}, u32[]{:S(2)}) %collective-permute-start.17) | collective-permute-done | bytes 16416 | tf_op jit(solution)/shard_map/ppermute | solution.py:250
  67.4 4.3 %collective-permute-start.20 = (f32[13,16,128]{2,1,0:T(8,128)S(1)}, f32[13,16,128]{2,1,0:T(8,128)S(1)}, u32[]{:S(2)}, u32[]{:S(2)}) collective-permute-start(f32[13,16,128]{2,1,0:T(8,128)S(1)} %get-tuple-element.94), channel_id=1, source_target_pairs={{0,4},{4,0},{8,12},{12,8},{1,5},{5,1},{9,13},{13,9},{2,6},{6,2},{1... | collective-permute-start | bytes 319496 | tf_op jit(solution)/shard_map/ppermute | solution.py:193
  72.1 2.0 %collective-permute-start.22 = (f32[13,16,128]{2,1,0:T(8,128)S(1)}, f32[13,16,128]{2,1,0:T(8,128)S(1)}, u32[]{:S(2)}, u32[]{:S(2)}) collective-permute-start(f32[13,16,128]{2,1,0:T(8,128)S(1)} %get-tuple-element.96), channel_id=1, source_target_pairs={{0,12},{4,8},{8,4},{12,0},{1,13},{5,9},{9,5},{13,1},{2,14},{6,10},... | collective-permute-start | bytes 319496 | tf_op jit(solution)/shard_map/ppermute | solution.py:193
  74.1 1.0 %collective-permute-start.18 = (f32[12,512]{1,0:T(8,128)S(1)}, f32[12,512]{1,0:T(8,128)S(1)}, u32[]{:S(2)}, u32[]{:S(2)}) collective-permute-start(f32[12,512]{1,0:T(8,128)S(1)} %get-tuple-element.91), channel_id=1, source_target_pairs={{0,4},{4,0},{8,12},{12,8},{1,5},{5,1},{9,13},{13,9},{2,6},{6,2},{1... | collective-permute-start | bytes 73736 | tf_op jit(solution)/shard_map/ppermute | solution.py:272
  75.2 0.7 collective-permute-start.19
  75.8 0.6 fusion.5
  76.4 3.2 %collective-permute-done.21.rest_2_ = f32[13,16,128]{2,1,0:T(8,128)S(1)} collective-permute-done((f32[13,16,128]{2,1,0:T(8,128)S(1)}, f32[13,16,128]{2,1,0:T(8,128)S(1)}, u32[]{:S(2)}, u32[]{:S(2)}) %collective-permute-start.21) | collective-permute-done | bytes 106528 | tf_op jit(solution)/shard_map/ppermute | solution.py:193
  79.9 1.2 %shard_map.90 = f32[12,8,512]{2,1,0:T(8,128)} custom-call(f32[12,8,512]{2,1,0:T(8,128)S(1)} %get-tuple-element.90.lam, f32[12,512]{1,0:T(8,128)S(1)} %collective-permute-done.18.edge_a, f32[12,512]{1,0:T(8,128)S(1)} %collective-permute-done.19.edge_b, f32[12,8,512]{2,1,0:T(8,128)S(1)} %get-tuple-element.56.me, f32[12,8,512]{2,1,0:T(8,128)S(1)} %get-tuple-element.57.mw, ...), custom_call_target="tpu_custom_call" | custom-call | tf_op jit(solution)/shard_map/pallas_call | solution.py:16
  (51 shorter events, 7.8 us)
Async XLA Ops:
  0.6 4.0 %copy-start = (f32[2,12,8,512]{3,2,1,0:T(8,128)S(1)}, f32[2,12,8,512]{3,2,1,0:T(8,128)}, u32[]{:S(2)}) copy-start(f32[2,12,8,512]{3,2,1,0:T(8,128)} %courant.1) | copy-start | bytes 1179652
  1.7 6.7 %collective-permute-start = (f32[13,8,256]{2,1,0:T(8,128)S(1)}, f32[13,8,256]{2,1,0:T(8,128)S(1)}, u32[]{:S(2)}, u32[]{:S(2)}) collective-permute-start(f32[13,8,256]{2,1,0:T(8,128)S(1)} %get-tuple-element.100), channel_id=1, source_target_pairs={{0,2},{2,0},{1,3},{3,1},{4,6},{6,4},{5,7},{7,5},{8,10},{10,8},{9,1... | collective-permute-start | bytes 319496 | tf_op jit(solution)/shard_map/ppermute | solution.py:207
  4.7 5.3 %collective-permute-start.1 = (f32[12,512]{1,0:T(8,128)S(1)}, f32[12,512]{1,0:T(8,128)S(1)}, u32[]{:S(2)}, u32[]{:S(2)}) collective-permute-start(f32[12,512]{1,0:T(8,128)S(1)} %bitcast.22), channel_id=1, source_target_pairs={{0,12},{4,0},{8,4},{12,8},{1,13},{5,1},{9,5},{13,9},{2,14},{6,2},{... | collective-permute-start | bytes 73736 | tf_op jit(solution)/shard_map/ppermute | solution.py:229
  8.4 1.5 %copy-start.2 = (f32[1,12,8,512]{3,2,1,0:T(8,128)S(1)}, f32[1,12,8,512]{3,2,1,0:T(8,128)}, u32[]{:S(2)}) copy-start(f32[1,12,8,512]{3,2,1,0:T(8,128)} %param.6) | copy-start | bytes 589828
  10.1 4.0 %collective-permute-start.2 = (f32[2,8,512]{2,1,0:T(8,128)S(1)}, f32[2,8,512]{2,1,0:T(8,128)S(1)}, u32[]{:S(2)}, u32[]{:S(2)}) collective-permute-start(f32[2,8,512]{2,1,0:T(8,128)S(1)} %get-tuple-element.51), channel_id=1, source_target_pairs={{0,2},{2,0},{1,3},{3,1},{4,6},{6,4},{5,7},{7,5},{8,10},{10,8},{9,1... | collective-permute-start | bytes 98312 | tf_op jit(solution)/shard_map/ppermute | solution.py:250
  14.2 4.0 %collective-permute-start.3 = (f32[12,512]{1,0:T(8,128)S(1)}, f32[12,512]{1,0:T(8,128)S(1)}, u32[]{:S(2)}, u32[]{:S(2)}) collective-permute-start(f32[12,512]{1,0:T(8,128)S(1)} %get-tuple-element.54), channel_id=1, source_target_pairs={{0,4},{4,0},{8,12},{12,8},{1,5},{5,1},{9,13},{13,9},{2,6},{6,2},{1... | collective-permute-start | bytes 73736 | tf_op jit(solution)/shard_map/ppermute | solution.py:272
  14.7 3.4 %collective-permute-start.4 = (f32[12,512]{1,0:T(8,128)S(1)}, f32[12,512]{1,0:T(8,128)S(1)}, u32[]{:S(2)}, u32[]{:S(2)}) collective-permute-start(f32[12,512]{1,0:T(8,128)S(1)} %get-tuple-element.55), channel_id=1, source_target_pairs={{0,0},{4,8},{8,4},{12,12},{1,1},{5,9},{9,5},{13,13},{2,2},{6,10},{... | collective-permute-start | bytes 73736 | tf_op jit(solution)/shard_map/ppermute | solution.py:273
  18.4 3.8 %collective-permute-start.5 = (f32[8,512]{1,0:T(8,128)S(1)}, f32[8,512]{1,0:T(8,128)S(1)}, u32[]{:S(2)}, u32[]{:S(2)}) collective-permute-start(f32[8,512]{1,0:T(8,128)S(1)} %get-tuple-element.63), channel_id=1, source_target_pairs={{0,2},{2,0},{1,3},{3,1},{4,6},{6,4},{5,7},{7,5},{8,10},{10,8},{9,1... | collective-permute-start | bytes 49160 | tf_op jit(solution)/shard_map/ppermute | solution.py:250
  22.2 7.1 %collective-permute-start.6 = (f32[12,512]{1,0:T(8,128)S(1)}, f32[12,512]{1,0:T(8,128)S(1)}, u32[]{:S(2)}, u32[]{:S(2)}) collective-permute-start(f32[12,512]{1,0:T(8,128)S(1)} %get-tuple-element.67), channel_id=1, source_target_pairs={{0,4},{4,0},{8,12},{12,8},{1,5},{5,1},{9,13},{13,9},{2,6},{6,2},{1... | collective-permute-start | bytes 73736 | tf_op jit(solution)/shard_map/ppermute | solution.py:272
  27.4 1.9 %collective-permute-start.7 = (f32[12,512]{1,0:T(8,128)S(1)}, f32[12,512]{1,0:T(8,128)S(1)}, u32[]{:S(2)}, u32[]{:S(2)}) collective-permute-start(f32[12,512]{1,0:T(8,128)S(1)} %get-tuple-element.68), channel_id=1, source_target_pairs={{0,0},{4,8},{8,4},{12,12},{1,1},{5,9},{9,5},{13,13},{2,2},{6,10},{... | collective-permute-start | bytes 73736 | tf_op jit(solution)/shard_map/ppermute | solution.py:273
  29.5 3.8 %collective-permute-start.8 = (f32[8,512]{1,0:T(8,128)S(1)}, f32[8,512]{1,0:T(8,128)S(1)}, u32[]{:S(2)}, u32[]{:S(2)}) collective-permute-start(f32[8,512]{1,0:T(8,128)S(1)} %get-tuple-element.70), channel_id=1, source_target_pairs={{0,2},{2,0},{1,3},{3,1},{4,6},{6,4},{5,7},{7,5},{8,10},{10,8},{9,1... | collective-permute-start | bytes 49160 | tf_op jit(solution)/shard_map/ppermute | solution.py:250
  33.4 7.9 %collective-permute-start.10 = (f32[12,512]{1,0:T(8,128)S(1)}, f32[12,512]{1,0:T(8,128)S(1)}, u32[]{:S(2)}, u32[]{:S(2)}) collective-permute-start(f32[12,512]{1,0:T(8,128)S(1)} %get-tuple-element.74), channel_id=1, source_target_pairs={{0,0},{4,8},{8,4},{12,12},{1,1},{5,9},{9,5},{13,13},{2,2},{6,10},{... | collective-permute-start | bytes 73736 | tf_op jit(solution)/shard_map/ppermute | solution.py:273
  34.1 9.1 %collective-permute-start.9 = (f32[12,512]{1,0:T(8,128)S(1)}, f32[12,512]{1,0:T(8,128)S(1)}, u32[]{:S(2)}, u32[]{:S(2)}) collective-permute-start(f32[12,512]{1,0:T(8,128)S(1)} %get-tuple-element.73), channel_id=1, source_target_pairs={{0,4},{4,0},{8,12},{12,8},{1,5},{5,1},{9,13},{13,9},{2,6},{6,2},{1... | collective-permute-start | bytes 73736 | tf_op jit(solution)/shard_map/ppermute | solution.py:272
  43.4 3.8 %collective-permute-start.11 = (f32[8,512]{1,0:T(8,128)S(1)}, f32[8,512]{1,0:T(8,128)S(1)}, u32[]{:S(2)}, u32[]{:S(2)}) collective-permute-start(f32[8,512]{1,0:T(8,128)S(1)} %get-tuple-element.76), channel_id=1, source_target_pairs={{0,2},{2,0},{1,3},{3,1},{4,6},{6,4},{5,7},{7,5},{8,10},{10,8},{9,1... | collective-permute-start | bytes 49160 | tf_op jit(solution)/shard_map/ppermute | solution.py:250
  47.3 4.0 %collective-permute-start.12 = (f32[12,512]{1,0:T(8,128)S(1)}, f32[12,512]{1,0:T(8,128)S(1)}, u32[]{:S(2)}, u32[]{:S(2)}) collective-permute-start(f32[12,512]{1,0:T(8,128)S(1)} %get-tuple-element.79), channel_id=1, source_target_pairs={{0,4},{4,0},{8,12},{12,8},{1,5},{5,1},{9,13},{13,9},{2,6},{6,2},{1... | collective-permute-start | bytes 73736 | tf_op jit(solution)/shard_map/ppermute | solution.py:272
  49.3 1.9 %collective-permute-start.13 = (f32[12,512]{1,0:T(8,128)S(1)}, f32[12,512]{1,0:T(8,128)S(1)}, u32[]{:S(2)}, u32[]{:S(2)}) collective-permute-start(f32[12,512]{1,0:T(8,128)S(1)} %get-tuple-element.80), channel_id=1, source_target_pairs={{0,0},{4,8},{8,4},{12,12},{1,1},{5,9},{9,5},{13,13},{2,2},{6,10},{... | collective-permute-start | bytes 73736 | tf_op jit(solution)/shard_map/ppermute | solution.py:273
  51.4 3.8 %collective-permute-start.14 = (f32[8,512]{1,0:T(8,128)S(1)}, f32[8,512]{1,0:T(8,128)S(1)}, u32[]{:S(2)}, u32[]{:S(2)}) collective-permute-start(f32[8,512]{1,0:T(8,128)S(1)} %get-tuple-element.82), channel_id=1, source_target_pairs={{0,2},{2,0},{1,3},{3,1},{4,6},{6,4},{5,7},{7,5},{8,10},{10,8},{9,1... | collective-permute-start | bytes 49160 | tf_op jit(solution)/shard_map/ppermute | solution.py:250
  55.3 6.0 %collective-permute-start.15 = (f32[12,512]{1,0:T(8,128)S(1)}, f32[12,512]{1,0:T(8,128)S(1)}, u32[]{:S(2)}, u32[]{:S(2)}) collective-permute-start(f32[12,512]{1,0:T(8,128)S(1)} %get-tuple-element.85), channel_id=1, source_target_pairs={{0,4},{4,0},{8,12},{12,8},{1,5},{5,1},{9,13},{13,9},{2,6},{6,2},{1... | collective-permute-start | bytes 73736 | tf_op jit(solution)/shard_map/ppermute | solution.py:272
  59.3 2.0 %collective-permute-start.16 = (f32[12,512]{1,0:T(8,128)S(1)}, f32[12,512]{1,0:T(8,128)S(1)}, u32[]{:S(2)}, u32[]{:S(2)}) collective-permute-start(f32[12,512]{1,0:T(8,128)S(1)} %get-tuple-element.86), channel_id=1, source_target_pairs={{0,0},{4,8},{8,4},{12,12},{1,1},{5,9},{9,5},{13,13},{2,2},{6,10},{... | collective-permute-start | bytes 73736 | tf_op jit(solution)/shard_map/ppermute | solution.py:273
  61.5 5.3 %copy-start.1 = (f32[1,12,64,128]{3,2,1,0:T(8,128)S(1)}, f32[1,12,64,128]{3,2,1,0:T(8,128)}, u32[]{:S(2)}) copy-start(f32[1,12,64,128]{3,2,1,0:T(8,128)} %param.9) | copy-start | bytes 1179652
  61.5 3.8 %collective-permute-start.17 = (f32[8,512]{1,0:T(8,128)S(1)}, f32[8,512]{1,0:T(8,128)S(1)}, u32[]{:S(2)}, u32[]{:S(2)}) collective-permute-start(f32[8,512]{1,0:T(8,128)S(1)} %get-tuple-element.88), channel_id=1, source_target_pairs={{0,2},{2,0},{1,3},{3,1},{4,6},{6,4},{5,7},{7,5},{8,10},{10,8},{9,1... | collective-permute-start | bytes 49160 | tf_op jit(solution)/shard_map/ppermute | solution.py:250
  65.4 0.7 copy-start.4
  65.4 9.7 %collective-permute-start.23 = (f32[8,256]{1,0:T(8,128)S(1)}, f32[8,256]{1,0:T(8,128)S(1)}, u32[]{:S(2)}, u32[]{:S(2)}) collective-permute-start(f32[8,256]{1,0:T(8,128)S(1)} %slice.12), channel_id=1, source_target_pairs={{0,2},{2,0},{1,3},{3,1},{4,6},{6,4},{5,7},{7,5},{8,10},{10,8},{9,1... | collective-permute-start | bytes 24584 | tf_op jit(solution)/shard_map/ppermute | solution.py:288
  66.1 0.7 copy-start.3
  67.4 9.0 %collective-permute-start.20 = (f32[13,16,128]{2,1,0:T(8,128)S(1)}, f32[13,16,128]{2,1,0:T(8,128)S(1)}, u32[]{:S(2)}, u32[]{:S(2)}) collective-permute-start(f32[13,16,128]{2,1,0:T(8,128)S(1)} %get-tuple-element.94), channel_id=1, source_target_pairs={{0,4},{4,0},{8,12},{12,8},{1,5},{5,1},{9,13},{13,9},{2,6},{6,2},{1... | collective-permute-start | bytes 319496 | tf_op jit(solution)/shard_map/ppermute | solution.py:193
  71.7 8.0 %collective-permute-start.21 = (f32[13,16,128]{2,1,0:T(8,128)S(1)}, f32[13,16,128]{2,1,0:T(8,128)S(1)}, u32[]{:S(2)}, u32[]{:S(2)}) collective-permute-start(f32[13,16,128]{2,1,0:T(8,128)S(1)} %get-tuple-element.95), channel_id=1, source_target_pairs={{0,8},{4,12},{8,0},{12,4},{1,9},{5,13},{9,1},{13,5},{2,10},{6,14},... | collective-permute-start | bytes 319496 | tf_op jit(solution)/shard_map/ppermute | solution.py:193
  72.1 7.5 %collective-permute-start.22 = (f32[13,16,128]{2,1,0:T(8,128)S(1)}, f32[13,16,128]{2,1,0:T(8,128)S(1)}, u32[]{:S(2)}, u32[]{:S(2)}) collective-permute-start(f32[13,16,128]{2,1,0:T(8,128)S(1)} %get-tuple-element.96), channel_id=1, source_target_pairs={{0,12},{4,8},{8,4},{12,0},{1,13},{5,9},{9,5},{13,1},{2,14},{6,10},... | collective-permute-start | bytes 319496 | tf_op jit(solution)/shard_map/ppermute | solution.py:193
  74.1 5.8 %collective-permute-start.18 = (f32[12,512]{1,0:T(8,128)S(1)}, f32[12,512]{1,0:T(8,128)S(1)}, u32[]{:S(2)}, u32[]{:S(2)}) collective-permute-start(f32[12,512]{1,0:T(8,128)S(1)} %get-tuple-element.91), channel_id=1, source_target_pairs={{0,4},{4,0},{8,12},{12,8},{1,5},{5,1},{9,13},{13,9},{2,6},{6,2},{1... | collective-permute-start | bytes 73736 | tf_op jit(solution)/shard_map/ppermute | solution.py:272
  75.2 4.7 %collective-permute-start.19 = (f32[12,512]{1,0:T(8,128)S(1)}, f32[12,512]{1,0:T(8,128)S(1)}, u32[]{:S(2)}, u32[]{:S(2)}) collective-permute-start(f32[12,512]{1,0:T(8,128)S(1)} %get-tuple-element.92), channel_id=1, source_target_pairs={{0,0},{4,8},{8,4},{12,12},{1,1},{5,9},{9,5},{13,13},{2,2},{6,10},{... | collective-permute-start | bytes 73736 | tf_op jit(solution)/shard_map/ppermute | solution.py:273
